TPU v7x, 128 devices: a whole 4x4x4 slice. The times are simulated.
128 devices in a mesh: section: 2 (over y_hi), shard: 8 (over x, core), replica: 8 (over z, y_lo).
Axes of the slice: x: 4, y: 4 (y_hi: 2, y_lo: 2; y = y_hi * 2 + y_lo), z: 4, core: 2. Of those that a mesh axis runs over, the one named last changes fastest.
Arguments:
- boundary: bfloat16 [2, 2, 8, 768, 1024], P('section', None, 'replica', 'shard'), may hold values from -6 to 6
- image_of_token: int32 [2, 8, 768], P(None, 'replica'), may hold values from 0 to 2, as said below
- ln1_gain: bfloat16 [2, 1024], P('section', 'shard'), may hold values from 0.5 to 1.5
- ln1_bias: bfloat16 [2, 1024], P('section', 'shard'), may hold values from -1.25 to 1.25
- w_qkv: bfloat16 [2, 1024, 3072], P('section', 'shard'), may hold values from -0.1875 to 0.1875
- qv_bias: bfloat16 [2, 2048], P('section', 'shard'), may hold values from -1.25 to 1.25
- w_out: bfloat16 [2, 1024, 1024], P('section', 'shard'), may hold values from -3 to 3
- out_bias: bfloat16 [2, 1024], P('section', 'shard'), may hold values from -1.25 to 1.25
- ln2_gain: bfloat16 [2, 1024], P('section', 'shard'), may hold values from 0.5 to 1.5
- ln2_bias: bfloat16 [2, 1024], P('section', 'shard'), may hold values from -1.25 to 1.25
- w_fc1: bfloat16 [2, 1024, 4096], P('section', 'shard'), may hold values from -0.1875 to 0.1875
- fc1_bias: bfloat16 [2, 4096], P('section', 'shard'), may hold values from -1.25 to 1.25
- w_fc2: bfloat16 [2, 4096, 1024], P('section', 'shard'), may hold values from -0.09375 to 0.09375
- fc2_bias: bfloat16 [2, 1024], P('section', 'shard'), may hold values from -1.25 to 1.25
Outputs:
- boundary_out: float32 [2, 2, 8, 768, 1024], P('section', None, 'replica', 'shard')
- grad_ln1_gain: float32 [2, 1024], P('section', 'shard')
- grad_ln1_bias: float32 [2, 1024], P('section', 'shard')
- grad_w_qkv: float32 [2, 1024, 3072], P('section', 'shard')
- grad_qv_bias: float32 [2, 2048], P('section', 'shard')
- grad_w_out: float32 [2, 1024, 1024], P('section', 'shard')
- grad_out_bias: float32 [2, 1024], P('section', 'shard')
- grad_ln2_gain: float32 [2, 1024], P('section', 'shard')
- grad_ln2_bias: float32 [2, 1024], P('section', 'shard')
- grad_w_fc1: float32 [2, 1024, 4096], P('section', 'shard')
- grad_fc1_bias: float32 [2, 4096], P('section', 'shard')
- grad_w_fc2: float32 [2, 4096, 1024], P('section', 'shard')
- grad_fc2_bias: float32 [2, 1024], P('section', 'shard')
Inputs may be any that keep to these rules, and one draw needn't show every extreme that they name: `image_of_token`: in every pack the image numbers start at 0, never fall and rise by one at each new image; every image of a pack but its first and its last has exactly 577 tokens, and those two have 1 to 577 tokens.
All inputs are finite; a program needn't handle non-finite values.
Results may differ from a plain program's by a relative error of at most 0.014.
Values may be sent and summed in bfloat16 or wider, within the bound.
A program may use at most 192 MiB of HBM per device.

v0:
```python
import math
import jax
import jax.numpy as jnp
from jax import lax
from jax.sharding import PartitionSpec as P

D = 1024
HEADS = 16
HEAD = 64
EPS = 1e-06
NEG = -1e30


def from_behind(x, axis, by):
    devices = lax.axis_size(axis)
    pairs = [(i, i + by) for i in range(devices) if 0 <= i + by < devices]
    return lax.ppermute(x, axis, pairs)


def layer_norm(resid_in, gain_vec, offset):
    centered = resid_in - jnp.mean(resid_in, axis=-1, keepdims=True)
    variance = jnp.mean(centered * centered, axis=-1, keepdims=True)
    return centered * lax.rsqrt(variance + EPS) * gain_vec + offset


def gelu_exact(inputs):
    return jax.nn.gelu(inputs, approximate=False)


def matmul(first_op, second_op):
    return jnp.dot(first_op, second_op, preferred_element_type=jnp.float32)


def matmul_t(first_op, second_op):
    return lax.dot_general(
        first_op, second_op, (((1,), (1,)), ((), ())), preferred_element_type=jnp.float32
    )


def over_rows(first_op, second_op):
    return lax.dot_general(
        first_op, second_op, (((0,), (0,)), ((), ())), preferred_element_type=jnp.float32
    )


def by_heads(matrix):
    return matrix.reshape(matrix.shape[0], HEADS, HEAD)


def masked_scores(queries, key_rows, query_ids, key_ids):
    scores = jnp.einsum(
        "qhd,khd->hqk", by_heads(queries), by_heads(key_rows), preferred_element_type=jnp.float32
    )
    scores = scores * (1.0 / math.sqrt(HEAD))
    allowed = (query_ids[:, None] == key_ids[None, :])[None]
    return jnp.where(allowed, scores, NEG)


def forward_block(weights, resid_in, image_ids, start_row):
    (
        ln1_gain,
        ln1_bias,
        w_qkv,
        qv_bias,
        w_out,
        out_bias,
        ln2_gain,
        ln2_bias,
        w_fc1,
        fc1_bias,
        w_fc2,
        fc2_bias,
    ) = weights
    token_count = resid_in.shape[0]
    query_ids = lax.dynamic_slice_in_dim(image_ids, start_row, token_count)
    normed_one = layer_norm(resid_in, ln1_gain, ln1_bias).astype(jnp.bfloat16)
    bias_full = jnp.concatenate([qv_bias[:D], jnp.zeros((D,), jnp.float32), qv_bias[D:]])
    projected = (matmul(normed_one, w_qkv) + bias_full).astype(jnp.bfloat16)
    kv_full = lax.all_gather(projected[:, D:], "shard", axis=0, tiled=True)
    scores = masked_scores(projected[:, :D], kv_full[:, :D], query_ids, image_ids)
    row_max = jnp.max(scores, axis=-1, keepdims=True)
    shifted = jnp.exp(scores - row_max)
    row_sum = jnp.sum(shifted, axis=-1, keepdims=True)
    probs_low = (shifted / row_sum).astype(jnp.bfloat16)
    log_total = row_max + jnp.log(row_sum)
    weighted = jnp.einsum(
        "hqk,khd->qhd", probs_low, by_heads(kv_full[:, D:]), preferred_element_type=jnp.float32
    )
    weighted = weighted.reshape(token_count, D).astype(jnp.bfloat16)
    resid_mid = resid_in + (matmul(weighted, w_out) + out_bias)
    normed_two = layer_norm(resid_mid, ln2_gain, ln2_bias).astype(jnp.bfloat16)
    hidden = matmul(normed_two, w_fc1) + fc1_bias
    activated = gelu_exact(hidden).astype(jnp.bfloat16)
    resid_out = resid_mid + (matmul(activated, w_fc2) + fc2_bias)
    stored = (
        resid_in,
        normed_one,
        projected,
        kv_full,
        log_total,
        weighted,
        resid_mid,
        normed_two,
        hidden,
        activated,
        image_ids,
    )
    return (resid_out, stored)


def backward_block(weights, stored, grad_out, start_row):
    (
        ln1_gain,
        ln1_bias,
        w_qkv,
        qv_bias,
        w_out,
        out_bias,
        ln2_gain,
        ln2_bias,
        w_fc1,
        fc1_bias,
        w_fc2,
        fc2_bias,
    ) = weights
    (
        resid_in,
        normed_one,
        projected,
        kv_full,
        log_total,
        weighted,
        resid_mid,
        normed_two,
        hidden,
        activated,
        image_ids,
    ) = stored
    token_count = resid_in.shape[0]
    score_scale = 1.0 / math.sqrt(HEAD)
    grad_mlp = grad_out.astype(jnp.bfloat16)
    d_activated = matmul_t(grad_mlp, w_fc2)
    d_hidden = jax.vjp(gelu_exact, hidden)[1](d_activated)[0].astype(jnp.bfloat16)
    d_normed_two = matmul_t(d_hidden, w_fc1)
    d_mid, d_ln2_gain, d_ln2_bias = jax.vjp(layer_norm, resid_mid, ln2_gain, ln2_bias)[1](
        d_normed_two
    )
    d_mid = grad_out + d_mid
    grad_attn = d_mid.astype(jnp.bfloat16)
    d_weighted = matmul_t(grad_attn, w_out).astype(jnp.bfloat16)
    query_ids = lax.dynamic_slice_in_dim(image_ids, start_row, token_count)
    scores = masked_scores(projected[:, :D], kv_full[:, :D], query_ids, image_ids)
    attn_probs = jnp.exp(scores - log_total)
    grad_heads = by_heads(d_weighted)
    query_heads = by_heads(projected[:, :D])
    d_probs = jnp.einsum(
        "qhd,khd->hqk", grad_heads, by_heads(kv_full[:, D:]), preferred_element_type=jnp.float32
    )
    d_scores = (
        attn_probs * (d_probs - jnp.sum(d_probs * attn_probs, axis=-1, keepdims=True))
    ).astype(jnp.bfloat16)
    probs_low = attn_probs.astype(jnp.bfloat16)
    d_queries = jnp.einsum(
        "hqk,khd->qhd", d_scores, by_heads(kv_full[:, :D]), preferred_element_type=jnp.float32
    )
    d_queries = d_queries.reshape(token_count, D) * score_scale
    d_keys = jnp.einsum("hqk,qhd->khd", d_scores, query_heads, preferred_element_type=jnp.float32)
    d_values = jnp.einsum("hqk,qhd->khd", probs_low, grad_heads, preferred_element_type=jnp.float32)
    d_kv = lax.psum_scatter(
        jnp.concatenate(
            [
                d_keys.reshape(token_count * lax.axis_size("shard"), D) * score_scale,
                d_values.reshape(token_count * lax.axis_size("shard"), D),
            ],
            axis=1,
        ).astype(jnp.bfloat16),
        "shard",
        scatter_dimension=0,
        tiled=True,
    ).astype(jnp.float32)
    d_projected = jnp.concatenate([d_queries, d_kv], axis=1).astype(jnp.bfloat16)
    d_normed_one = matmul_t(d_projected, w_qkv)
    d_resid, d_ln1_gain, d_ln1_bias = jax.vjp(layer_norm, resid_in, ln1_gain, ln1_bias)[1](
        d_normed_one
    )
    d_resid = d_mid + d_resid
    proj_wide = d_projected.astype(jnp.float32)
    d_qv_bias = jnp.concatenate(
        [jnp.sum(proj_wide[:, :D], axis=0), jnp.sum(proj_wide[:, 2 * D :], axis=0)]
    )
    vectors = (
        d_ln1_gain,
        d_ln1_bias,
        d_qv_bias,
        jnp.sum(grad_attn.astype(jnp.float32), axis=0),
        d_ln2_gain,
        d_ln2_bias,
        jnp.sum(d_hidden.astype(jnp.float32), axis=0),
        jnp.sum(grad_mlp.astype(jnp.float32), axis=0),
    )
    pair_terms = (
        (normed_one, d_projected),
        (weighted, grad_attn),
        (normed_two, d_hidden),
        (activated, grad_mlp),
    )
    return (d_resid, vectors, pair_terms)


def body(
    boundary,
    image_of_token,
    ln1_gain,
    ln1_bias,
    w_qkv,
    qv_bias,
    w_out,
    out_bias,
    ln2_gain,
    ln2_bias,
    w_fc1,
    fc1_bias,
    w_fc2,
    fc2_bias,
):
    shards = (
        ln1_gain[0],
        ln1_bias[0],
        w_qkv[0],
        qv_bias[0],
        w_out[0],
        out_bias[0],
        ln2_gain[0],
        ln2_bias[0],
        w_fc1[0],
        fc1_bias[0],
        w_fc2[0],
        fc2_bias[0],
    )
    gathered = (
        lax.all_gather(shards[0], "shard", axis=0, tiled=True),
        lax.all_gather(shards[1], "shard", axis=0, tiled=True),
        lax.all_gather(shards[2], "shard", axis=0, tiled=True),
        lax.all_gather(shards[3], "shard", axis=0, tiled=True),
        lax.all_gather(shards[4], "shard", axis=0, tiled=True),
        lax.all_gather(shards[5], "shard", axis=0, tiled=True),
        lax.all_gather(shards[6], "shard", axis=0, tiled=True),
        lax.all_gather(shards[7], "shard", axis=0, tiled=True),
        lax.all_gather(shards[8], "shard", axis=0, tiled=True),
        lax.all_gather(shards[9], "shard", axis=0, tiled=True),
        lax.all_gather(shards[10], "shard", axis=0, tiled=True),
        lax.all_gather(shards[11], "shard", axis=0, tiled=True),
    )
    weights = tuple(
        (member.astype(jnp.float32) if member.ndim == 1 else member for member in gathered)
    )
    section_zero = lax.axis_index("section") == 0
    local_data = boundary[0, :, 0].astype(jnp.float32)
    micro_count = local_data.shape[0]
    token_count = local_data.shape[1]
    start_row = lax.axis_index("shard") * token_count
    image_table = image_of_token[:, 0]
    empty_rows = jnp.zeros_like(local_data[0])
    stored_list = []
    resid_outs = []
    received = empty_rows
    for time_step in range(micro_count + 1):
        lower_input = local_data[time_step] if time_step < micro_count else empty_rows
        resid_in = jnp.where(section_zero, lower_input, received)
        image_ids = jnp.where(
            section_zero,
            image_table[min(time_step, micro_count - 1)],
            image_table[max(time_step - 1, 0)],
        )
        resid_out, stored = forward_block(weights, resid_in, image_ids, start_row)
        stored_list.append(stored)
        resid_outs.append(resid_out)
        if time_step < micro_count:
            received = from_behind(resid_out.astype(jnp.bfloat16), "section", 1).astype(jnp.float32)
    sent_back = empty_rows
    input_grads = []
    vector_sums = None
    pair_lists = [[], [], [], []]
    for time_step in range(micro_count + 1):
        lower_pick = time_step - 1 if time_step >= 1 else time_step + 1
        upper_pick = time_step + 1 if time_step < micro_count else time_step - 1
        stored = jax.tree.map(
            lambda lower_val, upper_val: jnp.where(section_zero, lower_val, upper_val),
            stored_list[lower_pick],
            stored_list[upper_pick],
        )
        upper_grad = local_data[time_step] if time_step < micro_count else empty_rows
        grad_out = jnp.where(section_zero, sent_back, upper_grad)
        d_resid, vectors, pair_terms = backward_block(weights, stored, grad_out, start_row)
        input_grads.append(d_resid)
        if vector_sums is None:
            vector_sums = vectors
        else:
            vector_sums = tuple((running + member for running, member in zip(vector_sums, vectors)))
        for pair_index in range(4):
            pair_lists[pair_index].append(pair_terms[pair_index])
        if time_step < micro_count:
            sent_back = from_behind(d_resid.astype(jnp.bfloat16), "section", -1).astype(jnp.float32)
    matrix_grads = []
    for pair_index in range(4):
        left_rows = jnp.concatenate(
            [entry_pair[0] for entry_pair in pair_lists[pair_index]], axis=0
        )
        right_rows = jnp.concatenate(
            [entry_pair[1] for entry_pair in pair_lists[pair_index]], axis=0
        )
        matrix_grads.append(over_rows(left_rows, right_rows))
    (
        d_ln1_gain,
        d_ln1_bias,
        d_qv_bias,
        d_out_bias,
        d_ln2_gain,
        d_ln2_bias,
        d_fc1_bias,
        d_fc2_bias,
    ) = vector_sums
    all_grads = (
        d_ln1_gain,
        d_ln1_bias,
        matrix_grads[0],
        d_qv_bias,
        matrix_grads[1],
        d_out_bias,
        d_ln2_gain,
        d_ln2_bias,
        matrix_grads[2],
        d_fc1_bias,
        matrix_grads[3],
        d_fc2_bias,
    )
    pieces = (
        lax.psum_scatter(all_grads[0], ("shard", "replica"), scatter_dimension=0, tiled=True),
        lax.psum_scatter(all_grads[1], ("shard", "replica"), scatter_dimension=0, tiled=True),
        lax.psum_scatter(all_grads[2], ("shard", "replica"), scatter_dimension=0, tiled=True),
        lax.psum_scatter(all_grads[3], ("shard", "replica"), scatter_dimension=0, tiled=True),
        lax.psum_scatter(all_grads[4], ("shard", "replica"), scatter_dimension=0, tiled=True),
        lax.psum_scatter(all_grads[5], ("shard", "replica"), scatter_dimension=0, tiled=True),
        lax.psum_scatter(all_grads[6], ("shard", "replica"), scatter_dimension=0, tiled=True),
        lax.psum_scatter(all_grads[7], ("shard", "replica"), scatter_dimension=0, tiled=True),
        lax.psum_scatter(all_grads[8], ("shard", "replica"), scatter_dimension=0, tiled=True),
        lax.psum_scatter(all_grads[9], ("shard", "replica"), scatter_dimension=0, tiled=True),
        lax.psum_scatter(all_grads[10], ("shard", "replica"), scatter_dimension=0, tiled=True),
        lax.psum_scatter(all_grads[11], ("shard", "replica"), scatter_dimension=0, tiled=True),
    )
    owner_part = (
        lax.all_gather(pieces[0].astype(jnp.bfloat16), "replica", axis=0, tiled=True).astype(
            jnp.float32
        ),
        lax.all_gather(pieces[1].astype(jnp.bfloat16), "replica", axis=0, tiled=True).astype(
            jnp.float32
        ),
        lax.all_gather(pieces[2].astype(jnp.bfloat16), "replica", axis=0, tiled=True).astype(
            jnp.float32
        ),
        lax.all_gather(pieces[3].astype(jnp.bfloat16), "replica", axis=0, tiled=True).astype(
            jnp.float32
        ),
        lax.all_gather(pieces[4].astype(jnp.bfloat16), "replica", axis=0, tiled=True).astype(
            jnp.float32
        ),
        lax.all_gather(pieces[5].astype(jnp.bfloat16), "replica", axis=0, tiled=True).astype(
            jnp.float32
        ),
        lax.all_gather(pieces[6].astype(jnp.bfloat16), "replica", axis=0, tiled=True).astype(
            jnp.float32
        ),
        lax.all_gather(pieces[7].astype(jnp.bfloat16), "replica", axis=0, tiled=True).astype(
            jnp.float32
        ),
        lax.all_gather(pieces[8].astype(jnp.bfloat16), "replica", axis=0, tiled=True).astype(
            jnp.float32
        ),
        lax.all_gather(pieces[9].astype(jnp.bfloat16), "replica", axis=0, tiled=True).astype(
            jnp.float32
        ),
        lax.all_gather(pieces[10].astype(jnp.bfloat16), "replica", axis=0, tiled=True).astype(
            jnp.float32
        ),
        lax.all_gather(pieces[11].astype(jnp.bfloat16), "replica", axis=0, tiled=True).astype(
            jnp.float32
        ),
    )
    stacked = jnp.stack(
        [
            jnp.where(section_zero, input_grads[micro_index + 1], resid_outs[micro_index + 1])
            for micro_index in range(micro_count)
        ]
    )
    boundary_out = stacked[None, :, None]
    return (boundary_out,) + tuple((member[None] for member in owner_part))


def solution(mesh):
    in_specs = (
        P("section", None, "replica", "shard", None),
        P(None, "replica", None),
        P("section", "shard"),
        P("section", "shard"),
        P("section", "shard", None),
        P("section", "shard"),
        P("section", "shard", None),
        P("section", "shard"),
        P("section", "shard"),
        P("section", "shard"),
        P("section", "shard", None),
        P("section", "shard"),
        P("section", "shard", None),
        P("section", "shard"),
    )
    out_specs = (
        P("section", None, "replica", "shard", None),
        P("section", "shard"),
        P("section", "shard"),
        P("section", "shard", None),
        P("section", "shard"),
        P("section", "shard", None),
        P("section", "shard"),
        P("section", "shard"),
        P("section", "shard"),
        P("section", "shard", None),
        P("section", "shard"),
        P("section", "shard", None),
        P("section", "shard"),
    )
    return jax.shard_map(body, mesh=mesh, in_specs=in_specs, out_specs=out_specs, check_vma=False)
```

profile of v0, /device:TPU:0, one launch (start us, length us, event | category | flops | bytes accessed | tf_op | source)
XLA Modules:
  0.0 2028.8 jit_solution(48523376486751329)
XLA Ops:
  8.0 10.8 all-gather
  18.7 8.2 all-gather.1
  28.0 9.5 all-gather.3
  38.5 14.6 all-gather.32.cloned.1.call-done
  60.0 8.6 all-gather.5
  68.6 8.9 all-gather.6
  77.5 8.6 all-gather.7
  86.1 8.9 all-gather.11
  95.1 11.5 all-gather.9
  122.6 41.9 %all-gather.36.cloned.1.call-done = bf16[1,1024,4096]{2,1,0:T(8,128)(2,1)} async-done(((bf16[1,128,4096]{2,1,0:T(8,128)(2,1)}), bf16[1,1024,4096]{2,1,0:T(8,128)(2,1)}) %all-gather.36.cloned.1.call-update) | async-done | bytes 8388624 | tf_op jit(solution)/shard_map/all_gather | solution.py:249
  164.6 9.2 fusion.120
  173.8 42.3 %all-gather.38.cloned.1.call-done = bf16[1,4096,1024]{2,1,0:T(8,128)(2,1)} async-done(((bf16[1,512,1024]{2,1,0:T(8,128)(2,1)}), bf16[1,4096,1024]{2,1,0:T(8,128)(2,1)}) %all-gather.38.cloned.1.call-update) | async-done | bytes 8388624 | tf_op jit(solution)/shard_map/all_gather | solution.py:251
  234.2 28.0 %all-gather.24.cloned.1.call-done = bf16[768,2048]{1,0:T(8,128)(2,1)} async-done(((bf16[96,2048]{1,0:T(8,128)(2,1)}), bf16[768,2048]{1,0:T(8,128)(2,1)}) %all-gather.24.cloned.1.call-update) | async-done | bytes 3145744 | tf_op jit(solution)/shard_map/all_gather | solution.py:79
  323.4 29.0 %reduce-scatter.22.cloned.1.call-done = bf16[96,2048]{1,0:T(8,128)(2,1)} async-done(((bf16[768,2048]{1,0:T(8,128)(2,1)}), bf16[96,2048]{1,0:T(8,128)(2,1)}) %reduce-scatter.22.cloned.1.call-update) | async-done | bytes 393232
  380.5 11.7 all-gather.26.cloned.1.call-done
  461.9 28.5 %reduce-scatter.24.cloned.1.call-done = bf16[96,2048]{1,0:T(8,128)(2,1)} async-done(((bf16[768,2048]{1,0:T(8,128)(2,1)}), bf16[96,2048]{1,0:T(8,128)(2,1)}) %reduce-scatter.24.cloned.1.call-update) | async-done | bytes 393232
  501.3 7.6 collective-permute-done.3
  509.6 7.1 convert_reduce_fusion
  545.1 11.7 fusion.84
  566.6 9.8 reduce-scatter.26.cloned.1.call-done
  577.7 9.8 fusion.72
  588.7 11.6 fusion.90
  613.5 283.8 %all-reduce.16 = (bf16[1024]{0:T(1024)(128)(2,1)S(1)}, bf16[1024]{0:T(1024)(128)(2,1)S(1)}, bf16[2048]{0:T(1024)(128)(2,1)S(1)}, bf16[1024]{0:T(1024)(128)(2,1)S...) all-reduce(f32[1024]{0:T(1024)S(1)} %add_add_fusion.15, ...), channel_id=17, replica_groups=mesh['section'=2,'shard'=8,'replica'=8] {'shard','replica'}, use_global_device_ids=true, to_apply=%region_43.44.clone | all-reduce | flops 12288 | bytes 73728
  899.7 17.9 all-reduce.17
  924.1 31.0 %reduce-scatter.18.cloned.1.call-done = f32[16,4096]{1,0:T(8,128)} async-done(((f32[1024,4096]{1,0:T(8,128)}), f32[16,4096]{1,0:T(8,128)}) %reduce-scatter.18.cloned.1.call-update) | async-done | bytes 262160 | tf_op jit(solution)/shard_map/reduce_scatter | solution.py:346
  960.9 291.3 %reduce-scatter.16.cloned.1.call-done = f32[16,1024]{1,0:T(8,128)} async-done(((f32[1024,1024]{1,0:T(8,128)}), f32[16,1024]{1,0:T(8,128)}) %reduce-scatter.16.cloned.1.call-update) | async-done | bytes 65552 | tf_op jit(solution)/shard_map/reduce_scatter | solution.py:342
  1253.0 31.9 %all_gather.100 = bf16[128,1024]{1,0:T(8,128)(2,1)S(1)} all-gather(bf16[16,1024]{1,0:T(8,128)(2,1)S(1)} %convert_element_type.334), channel_id=1, replica_groups=mesh['section'=2,'shard'=8,'replica'=8] {'replica'}, dimensions={0}, use_global_device_ids=true | all-gather | bytes 294912 | tf_op jit(solution)/shard_map/all_gather | solution.py:364
  1285.8 273.3 %reduce-scatter.14.cloned.1.call-done = f32[16,3072]{1,0:T(8,128)} async-done(((f32[1024,3072]{1,0:T(8,128)}), f32[16,3072]{1,0:T(8,128)}) %reduce-scatter.14.cloned.1.call-update) | async-done | bytes 196624 | tf_op jit(solution)/shard_map/reduce_scatter | solution.py:340
  1560.0 366.3 %reduce-scatter.20.cloned.1.call-done = f32[64,1024]{1,0:T(8,128)} async-done(((f32[4096,1024]{1,0:T(8,128)}), f32[64,1024]{1,0:T(8,128)}) %reduce-scatter.20.cloned.1.call-update) | async-done | bytes 262160 | tf_op jit(solution)/shard_map/reduce_scatter | solution.py:348
  1927.9 38.2 %all_gather.98 = bf16[128,3072]{1,0:T(8,128)(2,1)S(1)} all-gather(bf16[16,3072]{1,0:T(8,128)(2,1)S(1)} %convert_element_type.329), channel_id=1, replica_groups=mesh['section'=2,'shard'=8,'replica'=8] {'replica'}, dimensions={0}, use_global_device_ids=true | all-gather | bytes 884736 | tf_op jit(solution)/shard_map/all_gather | solution.py:358
  1967.4 9.9 all-gather.28.cloned.1.call-done
  1980.1 39.2 %all-gather.30.cloned.1.call-done = bf16[512,1024]{1,0:T(8,128)(2,1)} async-done(((bf16[64,1024]{1,0:T(8,128)(2,1)}), bf16[512,1024]{1,0:T(8,128)(2,1)}) %all-gather.30.cloned.1.call-update) | async-done | bytes 1048592 | tf_op jit(solution)/shard_map/all_gather | solution.py:382
  (645 shorter events, 287.4 us)
Async XLA Ops:
  7.2 45.9 %all-gather.32.cloned.1.call-start = ((), (), s32[]{:S(2)}) async-start(), calls=%async_computation.16 | async-start | bytes 7077888 | tf_op jit(solution)/shard_map/all_gather | solution.py:243
  7.9 99.7 %all-gather.22.cloned.1.call-start = ((), (), s32[]{:S(2)}) async-start(), calls=%async_computation.7 | async-start | bytes 3538944 | tf_op jit(solution)/shard_map/all_gather | solution.py:79
  26.9 204.0 %copy-start.84 = (f32[1,1024]{1,0:T(1,128)}, f32[1,1024]{1,0:T(1,128)S(1)}, u32[]{:S(2)}) copy-start(f32[1,1024]{1,0:T(1,128)S(1)} %convert_element_type.352) | copy-start | bytes 12292
  37.6 193.5 %copy-start.81 = (f32[3072]{0:T(1024)}, f32[3072]{0:T(1024)S(1)}, u32[]{:S(2)}) copy-start(f32[3072]{0:T(1024)S(1)} %pad_maximum_fusion.9) | copy-start | bytes 36868
  38.5 251.8 %copy-start.53 = (bf16[96,1024]{1,0:T(8,128)(2,1)}, bf16[96,1024]{1,0:T(8,128)(2,1)S(1)}, u32[]{:S(2)}) copy-start(bf16[96,1024]{1,0:T(8,128)(2,1)S(1)} %get-tuple-element.99) | copy-start | bytes 589828
  58.0 62.1 %all-gather.34.cloned.1.call-start = ((), (), s32[]{:S(2)}) async-start(), calls=%async_computation.17 | async-start | bytes 2359296 | tf_op jit(solution)/shard_map/all_gather | solution.py:245
  58.8 105.8 %all-gather.36.cloned.1.call-start = ((), (), s32[]{:S(2)}) async-start(), calls=%async_computation.18 | async-start | bytes 9437184 | tf_op jit(solution)/shard_map/all_gather | solution.py:249
  59.4 156.7 %all-gather.38.cloned.1.call-start = ((), (), s32[]{:S(2)}) async-start(), calls=%async_computation.19 | async-start | bytes 9437184 | tf_op jit(solution)/shard_map/all_gather | solution.py:251
  59.9 202.2 %all-gather.24.cloned.1.call-start = ((), (), s32[]{:S(2)}) async-start(), calls=%async_computation.8 | async-start | bytes 3538944 | tf_op jit(solution)/shard_map/all_gather | solution.py:79
  68.6 207.5 %copy-start.91 = (f32[1,1024]{1,0:T(1,128)}, f32[1,1024]{1,0:T(1,128)S(1)}, u32[]{:S(2)}) copy-start(f32[1,1024]{1,0:T(1,128)S(1)} %convert_element_type.354) | copy-start | bytes 12292
  86.1 191.1 %copy-start.95 = (f32[1,1024]{1,0:T(1,128)}, f32[1,1024]{1,0:T(1,128)S(1)}, u32[]{:S(2)}) copy-start(f32[1,1024]{1,0:T(1,128)S(1)} %convert_element_type.356) | copy-start | bytes 12292
  221.1 9.5 collective-permute-start
  233.1 119.2 %reduce-scatter.22.cloned.1.call-start = ((), (), s32[]{:S(2)}) async-start(), calls=%async_computation.20 | async-start | bytes 3538944
  285.2 12.9 collective-permute-start.2
  318.9 73.4 %all-gather.26.cloned.1.call-start = ((), (), s32[]{:S(2)}) async-start(), calls=%async_computation.9 | async-start | bytes 3538944 | tf_op jit(solution)/shard_map/all_gather | solution.py:79
  365.5 125.0 %reduce-scatter.24.cloned.1.call-start = ((), (), s32[]{:S(2)}) async-start(), calls=%async_computation.21 | async-start | bytes 3538944
  369.9 9.3 collective-permute-start.1
  454.6 121.8 %reduce-scatter.26.cloned.1.call-start = ((), (), s32[]{:S(2)}) async-start(), calls=%async_computation.22 | async-start | bytes 3538944
  499.8 9.1 collective-permute-start.3
  542.9 412.3 %reduce-scatter.18.cloned.1.call-start = ((), (), s32[]{:S(2)}) async-start(), calls=%async_computation.12 | async-start | bytes 17039360 | tf_op jit(solution)/shard_map/reduce_scatter | solution.py:346
  556.8 695.3 %reduce-scatter.16.cloned.1.call-start = ((), (), s32[]{:S(2)}) async-start(), calls=%async_computation.11 | async-start | bytes 4259840 | tf_op jit(solution)/shard_map/reduce_scatter | solution.py:342
  561.6 997.5 %reduce-scatter.14.cloned.1.call-start = ((), (), s32[]{:S(2)}) async-start(), calls=%async_computation.10 | async-start | bytes 12779520 | tf_op jit(solution)/shard_map/reduce_scatter | solution.py:340
  587.6 1338.7 %reduce-scatter.20.cloned.1.call-start = ((), (), s32[]{:S(2)}) async-start(), calls=%async_computation.14 | async-start | bytes 17039360 | tf_op jit(solution)/shard_map/reduce_scatter | solution.py:348
  600.3 1377.1 %all-gather.28.cloned.1.call-start = ((), (), s32[]{:S(2)}) async-start(), calls=%async_computation.13 | async-start | bytes 1179648 | tf_op jit(solution)/shard_map/all_gather | solution.py:376
  608.2 310.5 %copy-start.164 = (f32[96]{0:T(128)S(1)}, f32[96]{0:T(128)}, u32[]{:S(2)}) copy-start(f32[96]{0:T(128)} %get-tuple-element.124) | copy-start | bytes 1156
  608.3 310.8 %copy-start.40 = (bf16[96,4096]{1,0:T(8,128)(2,1)S(1)}, bf16[96,4096]{1,0:T(8,128)(2,1)}, u32[]{:S(2)}) copy-start(bf16[96,4096]{1,0:T(8,128)(2,1)} %get-tuple-element.95) | copy-start | bytes 2359300
  608.3 310.8 %copy-start.50 = (bf16[96,1024]{1,0:T(8,128)(2,1)S(1)}, bf16[96,1024]{1,0:T(8,128)(2,1)}, u32[]{:S(2)}) copy-start(bf16[96,1024]{1,0:T(8,128)(2,1)} %copy-done.49) | copy-start | bytes 589828
  608.3 310.8 %copy-start.90 = (f32[1,1024]{1,0:T(1,128)S(1)}, f32[1,1024]{1,0:T(1,128)}, u32[]{:S(2)}) copy-start(f32[1,1024]{1,0:T(1,128)} %copy-done.89) | copy-start | bytes 12292
  608.3 310.8 %copy-start.144 = (f32[96]{0:T(128)S(1)}, f32[96]{0:T(128)}, u32[]{:S(2)}) copy-start(f32[96]{0:T(128)} %copy-done.143) | copy-start | bytes 1156
  613.4 305.6 %copy-start.27 = (f32[96,1024]{1,0:T(8,128)S(1)}, f32[96,1024]{1,0:T(8,128)}, u32[]{:S(2)}) copy-start(f32[96,1024]{1,0:T(8,128)} %copy-done.26) | copy-start | bytes 1179652
  613.5 305.6 %copy-start.37 = (f32[96,1024]{1,0:T(8,128)S(1)}, f32[96,1024]{1,0:T(8,128)}, u32[]{:S(2)}) copy-start(f32[96,1024]{1,0:T(8,128)} %copy-done.36) | copy-start | bytes 1179652
  956.8 1062.5 %all-gather.30.cloned.1.call-start = ((), (), s32[]{:S(2)}) async-start(), calls=%async_computation.15 | async-start | bytes 1179648 | tf_op jit(solution)/shard_map/all_gather | solution.py:382
  (175 other events, 1820.4 us)
Sparse Core Ops, SparseCore 0:
  9.7 43.3 all-gather.31
  58.2 27.8 all-gather.21
  87.7 25.1 all-gather.33
  114.5 50.0 all-gather.35
  166.1 49.8 all-gather.37
  233.3 28.8 all-gather.23
  319.0 33.2 reduce-scatter.21
  365.6 26.5 all-gather.25
  454.7 35.7 reduce-scatter.23
  543.0 33.3 reduce-scatter.25
  578.8 376.3 reduce-scatter.17
  957.4 294.7 reduce-scatter.15
  1254.7 304.2 reduce-scatter.13
  1561.4 364.7 reduce-scatter.19
  1928.4 48.8 all-gather.27
  1978.9 40.2 all-gather.29
where the time goes:
time: 2030 us
  waiting for transfers between devices  1240 us (61%)
  blocking collectives  447 us (22%)
  matrix products  170 us (8%)
  local copies, waits for them, and re-layouts  81 us (4%)
  other arithmetic  58.5 us (3%)
  between operations  20.6 us (1%)
    reduce_scatter x1, waiting for transfers between devices, body(): lax.psum_scatter(all_grads[10], ('shard', 'replica'), scatter_dimension=0...  366 us
    unnamed x2, blocking collectives  302 us
    reduce_scatter x1, waiting for transfers between devices, body(): lax.psum_scatter(all_grads[4], ('shard', 'replica'), scatter_dimension=0,...  291 us
    reduce_scatter x1, waiting for transfers between devices, body(): lax.psum_scatter(all_grads[2], ('shard', 'replica'), scatter_dimension=0,...  273 us
    unnamed x19, waiting for transfers between devices  69.9 us
    dot_general x12, matrix products, matmul_t(): lax.dot_general(first_op, second_op, (((1,), (1,)), ((), ())), preferred_...  48.2 us
    all_gather x1, waiting for transfers between devices, body(): lax.all_gather(shards[10], 'shard', axis=0, tiled=True)  42.3 us
    dot_general x12, matrix products, matmul(): return jnp.dot(first_op, second_op, preferred_element_type=jnp.float32)  42.2 us
  transfers between devices with their start and end apart: 20, of which 17 were waited for; matrix products, arithmetic and copies ran while one was open for 6% of the time, Pallas kernels for 0%

commit v1 on v0

--- a/solution.py
+++ b/solution.py
@@ -248,7 +248,9 @@
         lax.all_gather(shards[7], "shard", axis=0, tiled=True),
         lax.all_gather(shards[8], "shard", axis=0, tiled=True),
         lax.all_gather(shards[9], "shard", axis=0, tiled=True),
-        lax.all_gather(shards[10], "shard", axis=0, tiled=True),
+        jnp.concatenate(
+            lax.all_to_all(jnp.stack([shards[10]] * lax.axis_size("shard")), "shard", 0, 0), axis=0
+        ),
         lax.all_gather(shards[11], "shard", axis=0, tiled=True),
     )
     weights = tuple(

time: 2030 us -> 2100 us (1.034)
  blocking collectives: 447 us -> 578 us
  waiting for transfers between devices: 1240 us -> 1150 us
    all_gather x1, blocking collectives: 8.59 us -> 140 us  [body(): lax.all_gather(shards[5], 'shard', axis=0, tiled=True)]
    all_gather x1 -> x0, waiting for transfers between devices: 42.3 us -> none  [body(): lax.all_gather(shards[10], 'shard', axis=0, tiled=True)]
    all_gather x1, waiting for transfers between devices: 41.9 us -> 0.02 us  [body(): lax.all_gather(shards[8], 'shard', axis=0, tiled=True)]
    unnamed x19 -> x18, waiting for transfers between devices: 69.9 us -> 69.4 us
  transfers between devices with their start and end apart: 20 -> 20, of which waited for: 17 -> 15; matrix products, arithmetic and copies ran while one was open for 6% -> 6% of each run, Pallas kernels for 0% -> 0%
where the time goes in v1:
time: 2100 us
  waiting for transfers between devices  1150 us (55%)
  blocking collectives  578 us (28%)
  matrix products  181 us (9%)
  local copies, waits for them, and re-layouts  85.4 us (4%)
  other arithmetic  58.2 us (3%)
    reduce_scatter x1, waiting for transfers between devices, body(): lax.psum_scatter(all_grads[10], ('shard', 'replica'), scatter_dimension=0...  366 us
    unnamed x2, blocking collectives  302 us
    reduce_scatter x1, waiting for transfers between devices, body(): lax.psum_scatter(all_grads[4], ('shard', 'replica'), scatter_dimension=0,...  292 us
    reduce_scatter x1, waiting for transfers between devices, body(): lax.psum_scatter(all_grads[2], ('shard', 'replica'), scatter_dimension=0,...  274 us
    all_gather x1, blocking collectives, body(): lax.all_gather(shards[5], 'shard', axis=0, tiled=True)  140 us
    unnamed x18, waiting for transfers between devices  69.4 us
    dot_general x12, matrix products, matmul_t(): lax.dot_general(first_op, second_op, (((1,), (1,)), ((), ())), preferred_...  53.9 us
    dot_general x12, matrix products, matmul(): return jnp.dot(first_op, second_op, preferred_element_type=jnp.float32)  47.1 us
  transfers between devices with their start and end apart: 20, of which 15 were waited for; matrix products, arithmetic and copies ran while one was open for 6% of the time, Pallas kernels for 0%

profile of v1, /device:TPU:0, one launch (start us, length us, event | category | flops | bytes accessed | tf_op | source)
XLA Modules:
  0.0 2096.8 jit_solution(2429496708842137626)
XLA Ops:
  8.0 10.8 all-gather
  18.7 8.2 all-gather.1
  28.0 9.5 all-gather.3
  38.0 15.2 all-gather.30.cloned.1.call-done
  68.9 140.5 %all-gather.5 = bf16[1,1024]{1,0:T(2,128)(2,1)S(1)} all-gather(bf16[1,128]{1,0:T(2,128)(2,1)S(1)} %copy-done.160), channel_id=7, replica_groups=mesh['section'=2,'shard'=8,'replica'=8] {'shard'}, dimensions={1}, use_global_device_ids=true | all-gather | bytes 2304 | tf_op jit(solution)/shard_map/all_gather | solution.py:246
  209.5 8.7 all-gather.6
  218.2 8.8 all-gather.7
  227.0 8.7 all-gather.10
  235.7 11.7 all-gather.9
  263.4 9.2 fusion.108
  291.0 28.5 %all-gather.22.cloned.1.call-done = bf16[768,2048]{1,0:T(8,128)(2,1)} async-done(((bf16[96,2048]{1,0:T(8,128)(2,1)}), bf16[768,2048]{1,0:T(8,128)(2,1)}) %all-gather.22.cloned.1.call-update) | async-done | bytes 3145744 | tf_op jit(solution)/shard_map/all_gather | solution.py:79
  340.2 7.0 fusion.273
  388.9 29.0 %reduce-scatter.22.cloned.1.call-done = bf16[96,2048]{1,0:T(8,128)(2,1)} async-done(((bf16[768,2048]{1,0:T(8,128)(2,1)}), bf16[96,2048]{1,0:T(8,128)(2,1)}) %reduce-scatter.22.cloned.1.call-update) | async-done | bytes 393232
  446.3 11.8 all-gather.24.cloned.1.call-done
  489.3 8.9 convert_reduce_fusion.1
  530.0 28.6 %reduce-scatter.24.cloned.1.call-done = bf16[96,2048]{1,0:T(8,128)(2,1)} async-done(((bf16[768,2048]{1,0:T(8,128)(2,1)}), bf16[96,2048]{1,0:T(8,128)(2,1)}) %reduce-scatter.24.cloned.1.call-update) | async-done | bytes 393232
  569.3 7.6 collective-permute-done.3
  577.6 7.1 convert_reduce_fusion
  613.1 11.7 fusion.72
  634.6 9.8 reduce-scatter.26.cloned.1.call-done
  645.8 9.8 fusion.60
  656.7 11.6 fusion.78
  681.6 283.5 %all-reduce.16 = (bf16[1024]{0:T(1024)(128)(2,1)S(1)}, bf16[1024]{0:T(1024)(128)(2,1)S(1)}, bf16[2048]{0:T(1024)(128)(2,1)S(1)}, bf16[1024]{0:T(1024)(128)(2,1)S...) all-reduce(f32[1024]{0:T(1024)S(1)} %add_add_fusion.15, ...), channel_id=16, replica_groups=mesh['section'=2,'shard'=8,'replica'=8] {'shard','replica'}, use_global_device_ids=true, to_apply=%region_43.44.clone | all-reduce | flops 12288 | bytes 73728
  967.4 18.2 all-reduce.17
  992.1 30.6 %reduce-scatter.18.cloned.1.call-done = f32[16,4096]{1,0:T(8,128)} async-done(((f32[1024,4096]{1,0:T(8,128)}), f32[16,4096]{1,0:T(8,128)}) %reduce-scatter.18.cloned.1.call-update) | async-done | bytes 262160 | tf_op jit(solution)/shard_map/reduce_scatter | solution.py:348
  1028.4 291.8 %reduce-scatter.16.cloned.1.call-done = f32[16,1024]{1,0:T(8,128)} async-done(((f32[1024,1024]{1,0:T(8,128)}), f32[16,1024]{1,0:T(8,128)}) %reduce-scatter.16.cloned.1.call-update) | async-done | bytes 65552 | tf_op jit(solution)/shard_map/reduce_scatter | solution.py:344
  1321.0 31.6 %all_gather.96 = bf16[128,1024]{1,0:T(8,128)(2,1)S(1)} all-gather(bf16[16,1024]{1,0:T(8,128)(2,1)S(1)} %convert_element_type.341), channel_id=1, replica_groups=mesh['section'=2,'shard'=8,'replica'=8] {'replica'}, dimensions={0}, use_global_device_ids=true | all-gather | bytes 294912 | tf_op jit(solution)/shard_map/all_gather | solution.py:366
  1353.5 274.2 %reduce-scatter.14.cloned.1.call-done = f32[16,3072]{1,0:T(8,128)} async-done(((f32[1024,3072]{1,0:T(8,128)}), f32[16,3072]{1,0:T(8,128)}) %reduce-scatter.14.cloned.1.call-update) | async-done | bytes 196624 | tf_op jit(solution)/shard_map/reduce_scatter | solution.py:342
  1628.6 365.8 %reduce-scatter.20.cloned.1.call-done = f32[64,1024]{1,0:T(8,128)} async-done(((f32[4096,1024]{1,0:T(8,128)}), f32[64,1024]{1,0:T(8,128)}) %reduce-scatter.20.cloned.1.call-update) | async-done | bytes 262160 | tf_op jit(solution)/shard_map/reduce_scatter | solution.py:350
  1996.0 38.2 %all_gather.94 = bf16[128,3072]{1,0:T(8,128)(2,1)S(1)} all-gather(bf16[16,3072]{1,0:T(8,128)(2,1)S(1)} %convert_element_type.336), channel_id=1, replica_groups=mesh['section'=2,'shard'=8,'replica'=8] {'replica'}, dimensions={0}, use_global_device_ids=true | all-gather | bytes 884736 | tf_op jit(solution)/shard_map/all_gather | solution.py:360
  2035.5 9.9 all-gather.26.cloned.1.call-done
  2048.2 39.1 %all-gather.28.cloned.1.call-done = bf16[512,1024]{1,0:T(8,128)(2,1)} async-done(((bf16[64,1024]{1,0:T(8,128)(2,1)}), bf16[512,1024]{1,0:T(8,128)(2,1)}) %all-gather.28.cloned.1.call-update) | async-done | bytes 1048592 | tf_op jit(solution)/shard_map/all_gather | solution.py:384
  (635 shorter events, 290.8 us)
Async XLA Ops:
  7.2 45.9 %all-gather.30.cloned.1.call-start = ((), (), s32[]{:S(2)}) async-start(), calls=%async_computation.17 | async-start | bytes 7077888 | tf_op jit(solution)/shard_map/all_gather | solution.py:243
  7.9 240.5 %all-gather.20.cloned.1.call-start = ((), (), s32[]{:S(2)}) async-start(), calls=%async_computation.8 | async-start | bytes 3538944 | tf_op jit(solution)/shard_map/all_gather | solution.py:79
  26.9 260.8 %copy-start.84 = (f32[1,1024]{1,0:T(1,128)}, f32[1,1024]{1,0:T(1,128)S(1)}, u32[]{:S(2)}) copy-start(f32[1,1024]{1,0:T(1,128)S(1)} %convert_element_type.360) | copy-start | bytes 12292
  37.6 250.3 %copy-start.81 = (f32[3072]{0:T(1024)}, f32[3072]{0:T(1024)S(1)}, u32[]{:S(2)}) copy-start(f32[3072]{0:T(1024)S(1)} %pad_maximum_fusion.9) | copy-start | bytes 36868
  57.1 191.1 %copy-start.38 = (bf16[96,3072]{1,0:T(8,128)(2,1)}, bf16[96,3072]{1,0:T(8,128)(2,1)S(1)}, u32[]{:S(2)}) copy-start(bf16[96,3072]{1,0:T(8,128)(2,1)S(1)} %fusion.53) | copy-start | bytes 1769476
  58.0 202.9 %all-gather.32.cloned.1.call-start = ((), (), s32[]{:S(2)}) async-start(), calls=%async_computation.18 | async-start | bytes 2359296 | tf_op jit(solution)/shard_map/all_gather | solution.py:245
  58.7 204.7 %all-gather.34.cloned.1.call-start = ((), (), s32[]{:S(2)}) async-start(), calls=%async_computation.19 | async-start | bytes 9437184 | tf_op jit(solution)/shard_map/all_gather | solution.py:249
  63.7 172.0 %copy-start.150 = (bf16[1,512]{1,0:T(2,128)(2,1)S(1)}, bf16[1,512]{1,0:T(2,128)(2,1)}, u32[]{:S(2)}) copy-start(bf16[1,512]{1,0:T(2,128)(2,1)} %param.25) | copy-start | bytes 3076
  63.7 183.7 %copy-start.130 = (s32[2,1,768]{2,1,0:T(1,128)S(1)}, s32[2,1,768]{2,1,0:T(1,128)}, u32[]{:S(2)}) copy-start(s32[2,1,768]{2,1,0:T(1,128)} %param.15) | copy-start | bytes 18436
  63.7 208.9 %all-to-all-start = ((bf16[8,512,1024]{2,1,0:T(8,128)(2,1)}), bf16[8,512,1024]{2,1,0:T(8,128)(2,1)}, u32[]{:S(2)}, u32[]{:S(2)}) async-start(bf16[8,512,1024]{2,1,0:T(8,128)(2,1)} %stack.12), calls=%async_computation | async-start | bytes 16777216 | tf_op jit(solution)/shard_map/all_to_all | solution.py:252
  68.9 250.6 %all-gather.22.cloned.1.call-start = ((), (), s32[]{:S(2)}) async-start(), calls=%async_computation.9 | async-start | bytes 3538944 | tf_op jit(solution)/shard_map/all_gather | solution.py:79
  277.8 9.5 collective-permute-start
  289.9 128.0 %reduce-scatter.22.cloned.1.call-start = ((), (), s32[]{:S(2)}) async-start(), calls=%async_computation.20 | async-start | bytes 3538944
  347.2 16.3 collective-permute-start.2
  384.4 73.6 %all-gather.24.cloned.1.call-start = ((), (), s32[]{:S(2)}) async-start(), calls=%async_computation.10 | async-start | bytes 3538944 | tf_op jit(solution)/shard_map/all_gather | solution.py:79
  431.3 127.3 %reduce-scatter.24.cloned.1.call-start = ((), (), s32[]{:S(2)}) async-start(), calls=%async_computation.21 | async-start | bytes 3538944
  435.7 9.3 collective-permute-start.1
  522.7 121.8 %reduce-scatter.26.cloned.1.call-start = ((), (), s32[]{:S(2)}) async-start(), calls=%async_computation.22 | async-start | bytes 3538944
  567.8 9.1 collective-permute-start.3
  610.9 411.8 %reduce-scatter.18.cloned.1.call-start = ((), (), s32[]{:S(2)}) async-start(), calls=%async_computation.13 | async-start | bytes 17039360 | tf_op jit(solution)/shard_map/reduce_scatter | solution.py:348
  624.8 695.3 %reduce-scatter.16.cloned.1.call-start = ((), (), s32[]{:S(2)}) async-start(), calls=%async_computation.12 | async-start | bytes 4259840 | tf_op jit(solution)/shard_map/reduce_scatter | solution.py:344
  629.6 998.1 %reduce-scatter.14.cloned.1.call-start = ((), (), s32[]{:S(2)}) async-start(), calls=%async_computation.11 | async-start | bytes 12779520 | tf_op jit(solution)/shard_map/reduce_scatter | solution.py:342
  655.6 1338.8 %reduce-scatter.20.cloned.1.call-start = ((), (), s32[]{:S(2)}) async-start(), calls=%async_computation.15 | async-start | bytes 17039360 | tf_op jit(solution)/shard_map/reduce_scatter | solution.py:350
  668.3 1377.1 %all-gather.26.cloned.1.call-start = ((), (), s32[]{:S(2)}) async-start(), calls=%async_computation.14 | async-start | bytes 1179648 | tf_op jit(solution)/shard_map/all_gather | solution.py:378
  676.3 310.4 %copy-start.164 = (f32[96]{0:T(128)S(1)}, f32[96]{0:T(128)}, u32[]{:S(2)}) copy-start(f32[96]{0:T(128)} %get-tuple-element.130) | copy-start | bytes 1156
  676.3 310.7 %copy-start.40 = (bf16[96,4096]{1,0:T(8,128)(2,1)S(1)}, bf16[96,4096]{1,0:T(8,128)(2,1)}, u32[]{:S(2)}) copy-start(bf16[96,4096]{1,0:T(8,128)(2,1)} %get-tuple-element.95) | copy-start | bytes 2359300
  676.3 310.7 %copy-start.50 = (bf16[96,1024]{1,0:T(8,128)(2,1)S(1)}, bf16[96,1024]{1,0:T(8,128)(2,1)}, u32[]{:S(2)}) copy-start(bf16[96,1024]{1,0:T(8,128)(2,1)} %copy-done.49) | copy-start | bytes 589828
  676.3 310.7 %copy-start.90 = (f32[1,1024]{1,0:T(1,128)S(1)}, f32[1,1024]{1,0:T(1,128)}, u32[]{:S(2)}) copy-start(f32[1,1024]{1,0:T(1,128)} %copy-done.89) | copy-start | bytes 12292
  676.3 310.7 %copy-start.144 = (f32[96]{0:T(128)S(1)}, f32[96]{0:T(128)}, u32[]{:S(2)}) copy-start(f32[96]{0:T(128)} %copy-done.143) | copy-start | bytes 1156
  681.5 305.5 %copy-start.27 = (f32[96,1024]{1,0:T(8,128)S(1)}, f32[96,1024]{1,0:T(8,128)}, u32[]{:S(2)}) copy-start(f32[96,1024]{1,0:T(8,128)} %copy-done.26) | copy-start | bytes 1179652
  681.5 305.5 %copy-start.37 = (f32[96,1024]{1,0:T(8,128)S(1)}, f32[96,1024]{1,0:T(8,128)}, u32[]{:S(2)}) copy-start(f32[96,1024]{1,0:T(8,128)} %copy-done.36) | copy-start | bytes 1179652
  1024.3 1063.0 %all-gather.28.cloned.1.call-start = ((), (), s32[]{:S(2)}) async-start(), calls=%async_computation.16 | async-start | bytes 1179648 | tf_op jit(solution)/shard_map/all_gather | solution.py:384
  (171 other events, 1896.0 us)
Sparse Core Ops, SparseCore 0:
  9.7 43.3 all-gather.29
  58.1 50.1 all-gather.19
  110.1 33.6 all-gather.31
  145.3 72.8 all-gather.33
  290.0 29.3 all-gather.21
  384.5 33.2 reduce-scatter.21
  431.4 26.5 all-gather.23
  522.8 35.7 reduce-scatter.23
  611.0 33.3 reduce-scatter.25
  646.7 375.9 reduce-scatter.17
  1025.0 295.1 reduce-scatter.15
  1322.6 305.0 reduce-scatter.13
  1630.2 364.1 reduce-scatter.19
  1996.5 48.8 all-gather.25
  2047.0 40.1 all-gather.27
